TPU v7x, 256 devices: a whole 4x4x8 slice. The times are simulated.
256 devices in a mesh: tp: 8 (over y, core), ex: 32 (over z, x).
Axes of the slice: x: 4, y: 4, z: 8, core: 2. Of those that a mesh axis runs over, the one named last changes fastest.
Arguments:
- token_ids: int32 [128, 128], P('ex'), may hold values from 0 to 128000, as said below
- attn_out: bfloat16 [128, 128, 4096], P('ex', None, 'tp'), may hold values from -6 to 6
- cotangent: bfloat16 [128, 128, 4096], P('ex', None, 'tp'), may hold values from -0.59765625 to 0.59765625
- basis_in: bfloat16 [4096, 4096], P('tp', 'ex'), may hold values from -0.09375 to 0.09375
- basis_out: bfloat16 [4096, 4096], P('tp', 'ex'), may hold values from -0.09375 to 0.09375
Outputs:
- corrections: float32 [4096, 4096], P('tp', 'ex')
Inputs may be any that keep to these rules, and one draw needn't show every extreme that they name: `token_ids`: 0 marks padding, which fills every sequence after its last real token; position 0 of every sequence holds 128000.
All inputs are finite; a program needn't handle non-finite values.
Results may differ from a plain program's by a relative error of at most 0.00084.
Values may be sent and summed in bfloat16 or wider, within the bound.
A program may use at most 128 MiB of HBM per device.

v0:
```python
import jax
import jax.numpy as jnp
from jax import lax
from jax.sharding import PartitionSpec as P


def on_device(token_ids, attn_out, cotangent, basis_in, basis_out):
    keep_mask = (token_ids != 0).astype(jnp.bfloat16)[:, :, None]
    masked = cotangent * keep_mask
    rows_in = lax.all_gather(basis_in, "ex", axis=1, tiled=True)
    rows_out = lax.all_gather(basis_out, "ex", axis=1, tiled=True)
    sliced = rows_in
    in_coeffs = lax.psum_scatter(
        jnp.einsum("dc,nld->cnl", sliced, attn_out, preferred_element_type=jnp.float32),
        "tp",
        scatter_dimension=0,
        tiled=True,
    ).astype(jnp.bfloat16)
    rotated_term = jnp.einsum("dc,nld->cnl", rows_out, masked, preferred_element_type=jnp.float32)
    out_coeffs = lax.psum(rotated_term, "tp").astype(jnp.bfloat16)
    examples = lax.axis_size("ex") * attn_out.shape[0]
    sliced = out_coeffs
    products = jnp.einsum("jnl,inl->nji", sliced, in_coeffs, preferred_element_type=jnp.float32)
    panel_sq = lax.psum_scatter(
        jnp.sum(products * products, axis=0), "ex", scatter_dimension=0, tiled=True
    )
    return panel_sq.T / examples


def solution(mesh):
    return jax.shard_map(
        on_device,
        mesh=mesh,
        in_specs=(
            P("ex", None),
            P("ex", None, "tp"),
            P("ex", None, "tp"),
            P("tp", "ex"),
            P("tp", "ex"),
        ),
        out_specs=P("tp", "ex"),
        check_vma=False,
    )
```

profile of v0, /device:TPU:1, one launch (start us, length us, event | category | flops | bytes accessed | tf_op | source)
XLA Modules:
  0.0 563.5 jit_solution(4918916889323088024)
XLA Ops:
  6.5 0.0 copy-start
  6.5 0.0 all-gather.5.cloned.1.call-start
  6.5 0.7 all-gather.5.cloned.1.call-update
  7.3 0.0 all-gather.3.cloned.1.call-start
  7.3 0.7 all-gather.3.cloned.1.call-update
  8.0 0.0 reduce-scatter.3.cloned.1.call-start
  8.1 85.5 %all-gather.5.cloned.1.call-done = bf16[512,4096]{1,0:T(8,128)(2,1)} async-done(((bf16[512,128]{1,0:T(8,128)(2,1)}), bf16[512,4096]{1,0:T(8,128)(2,1)}) %all-gather.5.cloned.1.call-update) | async-done | bytes 4194320 | tf_op jit(solution)/shard_map/all_gather | solution.py:10
  93.6 0.0 copy-done
  93.6 6.8 %fusion = f32[4096,4,128]{2,0,1:T(8,128)} fusion(bf16[4,128,512]{2,1,0:T(8,128)(2,1)S(1)} %copy-done, bf16[512,4096]{1,0:T(8,128)(2,1)} %all-gather.5.cloned.1.call-done), kind=kOutput, calls=%fused_computation.2 | convolution fusion | flops 2147483648 | bytes 13107200 | tf_op jit(solution)/shard_map/dc,nld->cnl/dot_general | solution.py:14
  100.4 0.0 copy-start.2
  100.4 0.0 copy-start.1
  100.4 0.0 reduce-scatter.3.cloned.1.call-update
  100.4 0.0 reduce-scatter.5.cloned.1.call-start
  100.4 0.6 copy-done.2
  101.1 78.4 %all-gather.3.cloned.1.call-done = bf16[512,4096]{1,0:T(8,128)(2,1)} async-done(((bf16[512,128]{1,0:T(8,128)(2,1)}), bf16[512,4096]{1,0:T(8,128)(2,1)}) %all-gather.3.cloned.1.call-update) | async-done | bytes 4194320 | tf_op jit(solution)/shard_map/all_gather | solution.py:11
  179.4 0.0 copy-done.1
  179.4 7.7 %convolution_bitcast_fusion = f32[4096,4,128]{2,0,1:T(8,128)} fusion(bf16[512,4096]{1,0:T(8,128)(2,1)} %all-gather.3.cloned.1.call-done, bf16[4,128,512]{2,1,0:T(8,128)(2,1)S(1)} %copy-done.1, bf16[4,128]{1,0:T(4,128)(2,1)S(1)} %compare_convert_fusion), kind=kOutput, calls=%fused_computation.1 | convolution fusion | flops 2147745792 | bytes 13108224 | tf_op jit(solution)/shard_map/dc,nld->cnl/dot_general | solution.py:19
  187.1 133.2 %all-reduce.1 = bf16[4096,4,128]{2,0,1:T(8,128)(2,1)} all-reduce(f32[4096,4,128]{2,0,1:T(8,128)} %convolution_bitcast_fusion), channel_id=1, replica_groups=mesh['tp'=8,'ex'=32] {'tp'}, use_global_device_ids=true, to_apply=%region_0.0 | all-reduce | flops 2097152 | bytes 12582912 | tf_op jit(solution)/shard_map/psum | solution.py:20
  320.4 0.0 reduce-scatter.3.cloned.1.call-done
  320.4 10.8 %multiply_reduce_fusion = f32[4096,512]{1,0:T(8,128)} fusion(bf16[4096,4,128]{2,0,1:T(8,128)(2,1)} %all-reduce.1, f32[512,4,128]{2,0,1:T(8,128)} %reduce-scatter.3.cloned.1.call-done), kind=kOutput, calls=%fused_computation | convolution fusion | flops 2162425856 | bytes 13631488 | tf_op jit(solution)/shard_map/jnl,inl->nji/dot_general | solution.py:23
  331.2 0.0 reduce-scatter.5.cloned.1.call-update
  331.2 224.0 %reduce-scatter.5.cloned.1.call-done = f32[128,512]{1,0:T(8,128)} async-done(((f32[4096,512]{1,0:T(8,128)}), f32[128,512]{1,0:T(8,128)}) %reduce-scatter.5.cloned.1.call-update) | async-done | bytes 262160 | tf_op jit(solution)/shard_map/reduce_scatter | solution.py:24
  555.1 1.0 multiply_bitcast_fusion
  556.1 0.8 copy.6
  (1 shorter events, 0.0 us)
Async XLA Ops:
  6.5 87.0 %copy-start = (bf16[4,128,512]{2,1,0:T(8,128)(2,1)S(1)}, bf16[4,128,512]{2,1,0:T(8,128)(2,1)}, u32[]{:S(2)}) copy-start(bf16[4,128,512]{2,1,0:T(8,128)(2,1)} %param.6) | copy-start | bytes 1572868
  6.5 87.0 %all-gather.5.cloned.1.call-start = ((), (), s32[]{:S(2)}) async-start(), calls=%async_computation.3 | async-start | bytes 4325376 | tf_op jit(solution)/shard_map/all_gather | solution.py:10
  7.3 172.1 %all-gather.3.cloned.1.call-start = ((), (), s32[]{:S(2)}) async-start(), calls=%async_computation.2 | async-start | bytes 4325376 | tf_op jit(solution)/shard_map/all_gather | solution.py:11
  8.0 312.4 %reduce-scatter.3.cloned.1.call-start = ((), (), s32[]{:S(2)}) async-start(), calls=%async_computation.4 | async-start | bytes 9437184 | tf_op jit(solution)/shard_map/reduce_scatter | solution.py:13
  100.4 0.7 copy-start.2
  100.4 79.0 %copy-start.1 = (bf16[4,128,512]{2,1,0:T(8,128)(2,1)S(1)}, bf16[4,128,512]{2,1,0:T(8,128)(2,1)}, u32[]{:S(2)}) copy-start(bf16[4,128,512]{2,1,0:T(8,128)(2,1)} %param.7) | copy-start | bytes 1572868
  100.4 454.7 %reduce-scatter.5.cloned.1.call-start = ((), (), s32[]{:S(2)}) async-start(), calls=%async_computation.5 | async-start | bytes 8650752 | tf_op jit(solution)/shard_map/reduce_scatter | solution.py:24
Sparse Core Ops, SparseCore 0:
  9.8 83.7 all-gather.4
  96.0 83.3 all-gather.2
  182.0 95.6 reduce-scatter.2
  331.3 223.7 reduce-scatter.4
where the time goes:
time: 567 us; the launch traced here: 563 us
  waiting for transfers between devices  389 us (69%)
  blocking collectives  133 us (23%)
  matrix products  25.3 us (4%)
  between operations  13.1 us (2%)
    reduce_scatter x1, waiting for transfers between devices, on_device(): lax.psum_scatter(jnp.sum(products * products, axis=0), 'ex', scatter_dime...  224 us
    psum x1, blocking collectives, on_device(): out_coeffs = lax.psum(rotated_term, 'tp').astype(jnp.bfloat16)  133 us
    all_gather x1, waiting for transfers between devices, on_device(): rows_in = lax.all_gather(basis_in, 'ex', axis=1, tiled=True)  85.5 us
    all_gather x1, waiting for transfers between devices, on_device(): rows_out = lax.all_gather(basis_out, 'ex', axis=1, tiled=True)  78.4 us
  transfers between devices with their start and end apart: 4, of which 3 were waited for; matrix products, arithmetic and copies ran while one was open for 3% of the time, Pallas kernels for 0%

commit v1 on v0

v1 whole, which is shorter than its diff:
```python
import functools

import jax
import jax.numpy as jnp
from jax import lax
from jax.experimental import pallas as pl
from jax.experimental.pallas import tpu as pltpu
from jax.sharding import PartitionSpec as P

MESH = pl.DeviceIdType.MESH
BF16 = jnp.bfloat16
F32 = jnp.float32
STEP = {(0, 0): 0, (0, 1): 1, (3, 0): 2, (1, 1): 3, (3, 1): 4, (1, 0): 5, (2, 0): 6, (2, 1): 7}


def remote(src, dst, send, recv, device):
    return pltpu.make_async_remote_copy(
        src_ref=src, dst_ref=dst, send_sem=send, recv_sem=recv, device_id=device, device_id_type=MESH
    )


def dot(a, b):
    return jnp.dot(a, b, preferred_element_type=F32)


def kernel(
    attn, cot, b_in, b_out, out,
    a, b, s1, relay, s2, fin, rq, acc, osend, orecv,
    local_sem, swap_send, swap_recv, b_send, b_recv, a_send, a_recv,
    s1_send, s1_recv, s2_send, s2_recv, r_send, r_recv, q_send, q_recv, o_send, o_recv,
):
    t, e = lax.axis_index("tp"), lax.axis_index("ex")
    y, c = lax.div(t, 2), lax.rem(t, 2)
    z, x = lax.div(e, 4), lax.rem(e, 4)
    xr, xl = (t, z * 4 + lax.rem(x + 1, 4)), (t, z * 4 + lax.rem(x + 3, 4))
    yr, yl = (lax.rem(y + 1, 4) * 2 + c, e), (lax.rem(y + 3, 4) * 2 + c, e)
    zr, zl = (t, lax.rem(z + 1, 8) * 4 + x), (t, lax.rem(z + 7, 8) * 4 + x)
    partner = (y * 2 + 1 - c, e)
    rr = (xr[0] * (1 - c) + yr[0] * c, xr[1] * (1 - c) + yr[1] * c)
    rl = (xl[0] * (1 - c) + yl[0] * c, xl[1] * (1 - c) + yl[1] * c)

    barrier = pltpu.get_barrier_semaphore()
    for device in (xr, xl, yr, yl, zr, zl, partner):
        pl.semaphore_signal(barrier, inc=1, device_id=device, device_id_type=MESH)
    pl.semaphore_wait(barrier, 7)

    half = pl.ds(pl.multiple_of(c * 512, 512), 512)
    other = pl.ds(pl.multiple_of((1 - c) * 512, 512), 512)

    def b_cols(zz):
        zz = lax.rem(zz + 16, 8)
        return lax.div(zz, 2), pl.ds(pl.multiple_of(lax.rem(zz, 2) * 128, 128), 128)

    own_pair, own_lanes = b_cols(z)

    def swap(mine_a, mine_b, theirs_a, theirs_b):
        def copies():
            yield pltpu.make_async_copy(mine_b, b.at[own_pair, half, own_lanes], local_sem.at[2])
            yield remote(theirs_b, b.at[own_pair, half, own_lanes], swap_send.at[2], swap_recv.at[2], partner)
            for u in range(2):
                yield pltpu.make_async_copy(mine_a.at[u], a.at[u, :, half], local_sem.at[u])
                yield remote(theirs_a.at[u], a.at[u, :, half], swap_send.at[u], swap_recv.at[u], partner)

        return copies

    @pl.when(c == 0)
    def _():
        for copy in swap(attn, b_in, cot, b_out)():
            copy.start()

    @pl.when(c == 1)
    def _():
        for copy in swap(cot, b_out, attn, b_in)():
            copy.start()

    def swapped_b():
        pltpu.make_async_copy(b_in, b.at[own_pair, half, own_lanes], local_sem.at[2]).wait()
        remote(b_in, b.at[own_pair, other, own_lanes], swap_send.at[2], swap_recv.at[2], partner).wait()

    def swapped_a(u):
        pltpu.make_async_copy(attn.at[u], a.at[u, :, half], local_sem.at[u]).wait()
        remote(attn.at[u], a.at[u, :, other], swap_send.at[u], swap_recv.at[u], partner).wait()

    def b_copy(hop, way, receive=False):
        origin = z - hop if way == 0 else z + hop
        if receive:
            origin = origin - 1 if way == 0 else origin + 1
        pair, lanes = b_cols(origin)
        rows = pl.ds(0, 1024) if hop < 3 else pl.ds(512 * way, 512)
        block = b.at[pair, rows, lanes]
        return remote(block, block, b_send.at[hop, way], b_recv.at[hop, way], zr if way == 0 else zl)

    a_moves = [(0, 2, 0), (1, 3, 1), (1, 4, 0), (0, 5, 1), (2, 6, 0), (3, 7, 1)]

    def a_copy(move):
        src, dst, way = a_moves[move]
        return remote(a.at[src], a.at[dst], a_send.at[move], a_recv.at[dst], xr if way == 0 else xl)

    swapped_b()
    for way in range(2):
        b_copy(0, way).start()
    swapped_a(0)
    a_copy(0).start()
    swapped_a(1)
    a_copy(1).start()
    a_copy(2).start()
    a_copy(3).start()
    for hop in range(4):
        for way in range(2):
            b_copy(hop, way, receive=True).wait_recv()
            if hop < 3:
                b_copy(hop + 1, way).start()
        if hop == 1:
            for move in range(2):
                a_copy(move).wait_recv()
                a_copy(move + 4).start()

    y_right, y_left, y_across = lax.rem(y + 1, 4), lax.rem(y + 3, 4), lax.rem(y + 2, 4)

    def relay_copy(k, way):
        return remote(s1.at[k, way], relay.at[k, way], s1_send.at[k, way], s1_recv.at[k, way], yr if way == 0 else yl)

    def fin_copy(k, way):
        return remote(s2.at[k, way], fin.at[k, way], s2_send.at[k, way], s2_recv.at[k, way], yr if way == 0 else yl)

    def r_copy(k, move):
        src, dst, way = [
            (rq.at[c, 0, k], rq.at[c, 3, k], 0),
            (rq.at[c, 0, k], rq.at[c, 1, k], 1),
            (rq.at[c, 3, k, pl.ds(0, 128)], rq.at[c, 2, k, pl.ds(0, 128)], 0),
            (rq.at[c, 1, k, pl.ds(128, 128)], rq.at[c, 2, k, pl.ds(128, 128)], 1),
        ][move]
        return remote(src, dst, r_send.at[k, move], r_recv.at[k, move], rr if way == 0 else rl)

    def q_copy(k, slot, receive=False):
        block = rq.at[1 - c if receive else c, slot, k]
        return remote(block, block, q_send.at[k, slot], q_recv.at[k, slot], partner)

    def tick(i, carry):
        def stage(lag, body):
            k = i - lag
            pl.when((k >= 0) & (k < 8))(functools.partial(body, k))

        def first(k):
            @pl.when(k >= 4)
            def _():
                remote(a.at[k], a.at[k], a_send.at[0], a_recv.at[k], xr).wait_recv()

            p = dot(a[k], b[y_across]).astype(BF16)
            s1[k, 0] = p[:128]
            s1[k, 1] = p[128:]
            for way in range(2):
                relay_copy(k, way).start()

        def second(k):
            for way, target in ((0, y_right), (1, y_left)):
                p = dot(a[k], b[target])
                relay_copy(k, way).wait_recv()
                if way == 0:
                    s2[k, 0, :128] = (p[:128] + relay[k, 0].astype(F32)).astype(BF16)
                    s2[k, 0, 128:] = p[128:].astype(BF16)
                else:
                    s2[k, 1, :128] = p[:128].astype(BF16)
                    s2[k, 1, 128:] = (p[128:] + relay[k, 1].astype(F32)).astype(BF16)
                fin_copy(k, way).start()

        def third(k):
            p = dot(a[k], b[y])
            for way in range(2):
                fin_copy(k, way).wait_recv()
            rq[c, 0, k] = (p + fin[k, 0].astype(F32) + fin[k, 1].astype(F32)).astype(BF16)
            r_copy(k, 0).start()
            r_copy(k, 1).start()
            q_copy(k, 0).start()

        def fourth(k):
            for move, slot in ((0, 3), (1, 1)):
                r_copy(k, move).wait_recv()
                r_copy(k, move + 2).start()
                q_copy(k, slot).start()

        def fifth(k):
            r_copy(k, 2).wait_recv()
            r_copy(k, 3).wait_recv()
            q_copy(k, 2).start()

        stage(0, first)
        stage(1, second)
        stage(2, third)
        stage(3, fourth)
        stage(4, fifth)
        return carry

    lax.fori_loop(0, 12, tick, 0)

    lanes = pl.ds(pl.multiple_of(c * 128, 128), 128)

    def take(k, carry):
        for slot in range(4):
            q_copy(k, slot, receive=True).wait_recv()
        return carry

    lax.fori_loop(0, 8, take, 0)
    acc[...] = jnp.zeros_like(acc)
    for ds in range(4):
        for u in range(2):

            def example(h, carry, ds=ds, u=u):
                rows = pl.ds(pl.multiple_of(h * 128, 128), 128)
                left = jnp.concatenate(
                    [rq[0, dx, STEP[(ds - dx) % 4, u], rows, lanes] for dx in range(4)], axis=1
                )
                for dy in range(4):
                    right = rq[1, dy, STEP[ds, u], rows, :]
                    coeff = lax.dot_general(left, right, (((0,), (0,)), ((), ())), preferred_element_type=F32)
                    acc[dy] += coeff * coeff
                return carry

            lax.fori_loop(0, 2, example, 0)

    def part(d, upper):
        zz = lax.rem(z + d + 16, 8)
        slot = lax.rem(lax.div(zz, 2) - y + 4, 4)
        return acc[slot, 256 * upper : 256 * upper + 256, pl.ds(pl.multiple_of(lax.rem(zz, 2) * 128, 128), 128)]

    def o_copy(way, i):
        return remote(osend.at[way, i], orecv.at[way, i], o_send.at[way, i], o_recv.at[way, i], zr if way == 0 else zl)

    for i in range(7):
        for way in range(2):
            d = 4 - (i + 1) // 2
            block = part(d if way == 0 else -d, (i % 2) ^ way)
            if i >= 2:
                o_copy(way, i - 2).wait_recv()
                block = block + orecv[way, i - 2]
            osend[way, i] = block
            o_copy(way, i).start()
    for i in (5, 6):
        for way in range(2):
            o_copy(way, i).wait_recv()
    for upper in range(2):
        total = (part(0, upper) + orecv[0, 6 - upper] + orecv[1, 5 + upper]) * (1.0 / 128.0)
        for s in range(2):
            place = lax.rem(x + 2 * upper + s, 4)
            out[pl.ds(pl.multiple_of(place * 128, 128), 128), :] = total[128 * s : 128 * s + 128]

    for hop in range(4):
        for way in range(2):
            b_copy(hop, way).wait_send()
    for move in range(6):
        a_copy(move).wait_send()

    def sent(k, carry):
        for way in range(2):
            relay_copy(k, way).wait_send()
            fin_copy(k, way).wait_send()
        for move in range(4):
            r_copy(k, move).wait_send()
            q_copy(k, move).wait_send()
        return carry

    lax.fori_loop(0, 8, sent, 0)
    for i in range(7):
        for way in range(2):
            o_copy(way, i).wait_send()


def on_device(token_ids, attn_out, cotangent, basis_in, basis_out):
    keep_mask = (token_ids != 0).astype(BF16)[:, :, None]
    masked = (cotangent * keep_mask).reshape(2, 256, 512)
    dma = pltpu.SemaphoreType.DMA
    return pl.pallas_call(
        kernel,
        out_shape=jax.ShapeDtypeStruct((512, 128), F32),
        in_specs=[pl.BlockSpec(memory_space=pl.ANY)] * 4,
        out_specs=pl.BlockSpec(memory_space=pltpu.VMEM),
        scratch_shapes=[
            pltpu.VMEM((8, 256, 1024), BF16),
            pltpu.VMEM((4, 1024, 256), BF16),
            pltpu.VMEM((8, 2, 128, 256), BF16),
            pltpu.VMEM((8, 2, 128, 256), BF16),
            pltpu.VMEM((8, 2, 256, 256), BF16),
            pltpu.VMEM((8, 2, 256, 256), BF16),
            pltpu.VMEM((2, 4, 8, 256, 256), BF16),
            pltpu.VMEM((4, 512, 256), F32),
            pltpu.VMEM((2, 7, 256, 128), F32),
            pltpu.VMEM((2, 7, 256, 128), F32),
            dma((3,)), dma((3,)), dma((3,)),
            dma((4, 2)), dma((4, 2)),
            dma((6,)), dma((8,)),
            dma((8, 2)), dma((8, 2)), dma((8, 2)), dma((8, 2)),
            dma((8, 4)), dma((8, 4)), dma((8, 4)), dma((8, 4)),
            dma((2, 7)), dma((2, 7)),
        ],
        compiler_params=pltpu.CompilerParams(
            collective_id=0, has_side_effects=True, vmem_limit_bytes=48 * 1024 * 1024
        ),
    )(attn_out.reshape(2, 256, 512), masked, basis_in, basis_out)


def solution(mesh):
    return jax.shard_map(
        on_device,
        mesh=mesh,
        in_specs=(
            P("ex", None),
            P("ex", None, "tp"),
            P("ex", None, "tp"),
            P("tp", "ex"),
            P("tp", "ex"),
        ),
        out_specs=P("tp", "ex"),
        check_vma=False,
    )
```

time: 567 us -> 125 us (0.22)
  waiting for transfers between devices: 389 us -> 0 us
  blocking collectives: 133 us -> 0 us
  Pallas kernels: 0 us -> 122 us
  matrix products: 25.3 us -> 0 us
  between operations: 13.1 us -> 0.04 us
    reduce_scatter x2 -> x0, waiting for transfers between devices: 224 us -> none  [the longest x1 224 us: on_device(): lax.psum_scatter(jnp.sum(products * products, axis=0), 'ex', scatter_dime...]
    all_gather x2 -> x0, waiting for transfers between devices: 164 us -> none  [the longest x1 85.5 us: on_device(): rows_in = lax.all_gather(basis_in, 'ex', axis=1, tiled=True)]
    psum x1 -> x0, blocking collectives: 133 us -> none  [on_device(): out_coeffs = lax.psum(rotated_term, 'tp').astype(jnp.bfloat16)]
    pallas_call x0 -> x1, Pallas kernels: none -> 122 us  [on_device(): pl.pallas_call(kernel, out_shape=jax.ShapeDtypeStruct((512, 128), F32), i...]
    dot_general x3 -> x0, matrix products: 25.3 us -> none  [the longest x1 10.8 us: on_device(): jnp.einsum('jnl,inl->nji', sliced, in_coeffs, preferred_element_type=jnp....]
  transfers between devices with their start and end apart: 4 -> 0, of which waited for: 3 -> 0; matrix products, arithmetic and copies ran while one was open for 3% -> 0% of each run, Pallas kernels for 0% -> 0%
where the time goes in v1:
time: 125 us
  Pallas kernels  122 us (98%)
  other arithmetic  1.93 us (2%)
    pallas_call x1, Pallas kernels, on_device(): pl.pallas_call(kernel, out_shape=jax.ShapeDtypeStruct((512, 128), F32), i...  122 us

profile of v1, /device:TPU:1, one launch (start us, length us, event | category | flops | bytes accessed | tf_op | source)
XLA Modules:
  0.0 125.1 jit_solution(4317214311742876009)
XLA Ops:
  0.0 0.7 compare_convert_fusion
  0.7 0.0 copy-start
  0.7 0.0 copy-start.1
  0.7 0.0 copy-start.2
  0.7 1.2 broadcast_multiply_fusion
  1.9 0.0 copy-done
  2.0 0.0 copy-done.1
  2.0 0.0 copy-done.2
  2.0 122.4 %shard_map.55 = f32[512,128]{1,0:T(8,128)S(1)} custom-call(bf16[2,256,512]{2,1,0:T(8,128)(2,1)S(1)} %bitcast.3, bf16[2,256,512]{2,1,0:T(8,128)(2,1)S(1)} %bitcast.2, bf16[512,128]{1,0:T(8,128)(2,1)S(1)} %copy-done.1, bf16[512,128]{1,0:T(8,128)(2,1)S(1)} %copy-done.2), custom_call_target="tpu_custom_call" | custom-call | tf_op jit(solution)/shard_map/pallas_call | solution.py:272
  124.3 0.7 copy.7
Async XLA Ops:
  0.7 1.3 %copy-start = (bf16[4,128,512]{2,1,0:T(8,128)(2,1)S(1)}, bf16[4,128,512]{2,1,0:T(8,128)(2,1)}, u32[]{:S(2)}) copy-start(bf16[4,128,512]{2,1,0:T(8,128)(2,1)} %param.6) | copy-start | bytes 1572868
  0.7 1.3 %copy-start.1 = (bf16[512,128]{1,0:T(8,128)(2,1)S(1)}, bf16[512,128]{1,0:T(8,128)(2,1)}, u32[]{:S(2)}) copy-start(bf16[512,128]{1,0:T(8,128)(2,1)} %b_in.1) | copy-start | bytes 393220
  0.7 1.3 %copy-start.2 = (bf16[512,128]{1,0:T(8,128)(2,1)S(1)}, bf16[512,128]{1,0:T(8,128)(2,1)}, u32[]{:S(2)}) copy-start(bf16[512,128]{1,0:T(8,128)(2,1)} %b_out.1) | copy-start | bytes 393220

commit v2 on v1

--- a/solution.py
+++ b/solution.py
@@ -11,6 +11,7 @@
 BF16 = jnp.bfloat16
 F32 = jnp.float32
 STEP = {(0, 0): 0, (0, 1): 1, (3, 0): 2, (1, 1): 3, (3, 1): 4, (1, 0): 5, (2, 0): 6, (2, 1): 7}
+LAG = 2
 
 
 def remote(src, dst, send, recv, device):
@@ -24,7 +25,7 @@
 
 
 def kernel(
-    attn, cot, b_in, b_out, out,
+    tokens, attn, cot, b_in, b_out, out,
     a, b, s1, relay, s2, fin, rq, acc, osend, orecv,
     local_sem, swap_send, swap_recv, b_send, b_recv, a_send, a_recv,
     s1_send, s1_recv, s2_send, s2_recv, r_send, r_recv, q_send, q_recv, o_send, o_recv,
@@ -96,15 +97,28 @@
         src, dst, way = a_moves[move]
         return remote(a.at[src], a.at[dst], a_send.at[move], a_recv.at[dst], xr if way == 0 else xl)
 
+    def take_a(u):
+        swapped_a(u)
+
+        @pl.when(c == 1)
+        def _():
+            square = (128, 128)
+            diagonal = lax.broadcasted_iota(jnp.int32, square, 0) == lax.broadcasted_iota(jnp.int32, square, 1)
+            for h in range(2):
+                keep = jnp.where(tokens[2 * u + h : 2 * u + h + 1, :] != 0, 1.0, 0.0).astype(F32)
+                column = jnp.sum(jnp.where(diagonal, keep, 0.0), axis=1, keepdims=True).astype(BF16)
+                a[u, 128 * h : 128 * h + 128, :] = a[u, 128 * h : 128 * h + 128, :] * column
+
     swapped_b()
     for way in range(2):
         b_copy(0, way).start()
-    swapped_a(0)
+    take_a(0)
     a_copy(0).start()
-    swapped_a(1)
+    take_a(1)
     a_copy(1).start()
     a_copy(2).start()
     a_copy(3).start()
+    acc[...] = jnp.zeros_like(acc)
     for hop in range(4):
         for way in range(2):
             b_copy(hop, way, receive=True).wait_recv()
@@ -136,9 +150,17 @@
         block = rq.at[1 - c if receive else c, slot, k]
         return remote(block, block, q_send.at[k, slot], q_recv.at[k, slot], partner)
 
+    def q_copy_in(k, slot):
+        block = rq.at[0, slot, k, pl.ds(128, 128)]
+        return remote(block, block, q_send.at[k, slot], q_recv.at[k, slot], partner)
+
+    def hand_over(k, slot, act):
+        pl.when(c == 0)(lambda: getattr(q_copy_in(k, slot), act)())
+        pl.when(c == 1)(lambda: getattr(q_copy(k, slot), act)())
+
     def tick(i, carry):
         def stage(lag, body):
-            k = i - lag
+            k = i - lag * LAG
             pl.when((k >= 0) & (k < 8))(functools.partial(body, k))
 
         def first(k):
@@ -168,21 +190,30 @@
             p = dot(a[k], b[y])
             for way in range(2):
                 fin_copy(k, way).wait_recv()
-            rq[c, 0, k] = (p + fin[k, 0].astype(F32) + fin[k, 1].astype(F32)).astype(BF16)
+            total = p + fin[k, 0].astype(F32) + fin[k, 1].astype(F32)
+
+            @pl.when(c == 0)
+            def _():
+                rq[0, 0, k] = total.T.astype(BF16)
+
+            @pl.when(c == 1)
+            def _():
+                rq[1, 0, k] = total.astype(BF16)
+
             r_copy(k, 0).start()
             r_copy(k, 1).start()
-            q_copy(k, 0).start()
+            hand_over(k, 0, "start")
 
         def fourth(k):
             for move, slot in ((0, 3), (1, 1)):
                 r_copy(k, move).wait_recv()
                 r_copy(k, move + 2).start()
-                q_copy(k, slot).start()
+                hand_over(k, slot, "start")
 
         def fifth(k):
             r_copy(k, 2).wait_recv()
             r_copy(k, 3).wait_recv()
-            q_copy(k, 2).start()
+            hand_over(k, 2, "start")
 
         stage(0, first)
         stage(1, second)
@@ -191,50 +222,86 @@
         stage(4, fifth)
         return carry
 
-    lax.fori_loop(0, 12, tick, 0)
+    lax.fori_loop(0, 8 + 4 * LAG, tick, 0)
+
+    odd = lax.rem(z, 2)
 
     lanes = pl.ds(pl.multiple_of(c * 128, 128), 128)
 
-    def take(k, carry):
-        for slot in range(4):
-            q_copy(k, slot, receive=True).wait_recv()
-        return carry
-
-    lax.fori_loop(0, 8, take, 0)
-    acc[...] = jnp.zeros_like(acc)
-    for ds in range(4):
-        for u in range(2):
-
-            def example(h, carry, ds=ds, u=u):
-                rows = pl.ds(pl.multiple_of(h * 128, 128), 128)
-                left = jnp.concatenate(
-                    [rq[0, dx, STEP[(ds - dx) % 4, u], rows, lanes] for dx in range(4)], axis=1
-                )
-                for dy in range(4):
-                    right = rq[1, dy, STEP[ds, u], rows, :]
-                    coeff = lax.dot_general(left, right, (((0,), (0,)), ((), ())), preferred_element_type=F32)
-                    acc[dy] += coeff * coeff
+    def product(pair):
+        slot = lax.rem(pair - y + 4, 4)
+
+        @pl.when(c == 0)
+        def _():
+            def take(k, carry):
+                q_copy(k, slot, receive=True).wait_recv()
                 return carry
 
-            lax.fori_loop(0, 2, example, 0)
+            lax.fori_loop(0, 8, take, 0)
+
+        for ds in range(4):
+            for u in range(2):
+                squares = 0.0
+                for h in range(2):
+                    rows = slice(128 * h, 128 * h + 128)
+                    left = jnp.concatenate(
+                        [rq[0, dx, STEP[(ds - dx) % 4, u], lanes, rows] for dx in range(4)], axis=0
+                    )
+                    coeff = dot(left, rq[1, slot, STEP[ds, u], rows, :])
+                    squares = squares + coeff * coeff
+                acc[pair] += squares
 
     def part(d, upper):
         zz = lax.rem(z + d + 16, 8)
-        slot = lax.rem(lax.div(zz, 2) - y + 4, 4)
-        return acc[slot, 256 * upper : 256 * upper + 256, pl.ds(pl.multiple_of(lax.rem(zz, 2) * 128, 128), 128)]
+        return acc[lax.div(zz, 2), 256 * upper : 256 * upper + 256, pl.ds(pl.multiple_of(lax.rem(zz, 2) * 128, 128), 128)]
 
     def o_copy(way, i):
         return remote(osend.at[way, i], orecv.at[way, i], o_send.at[way, i], o_recv.at[way, i], zr if way == 0 else zl)
 
-    for i in range(7):
-        for way in range(2):
-            d = 4 - (i + 1) // 2
-            block = part(d if way == 0 else -d, (i % 2) ^ way)
-            if i >= 2:
-                o_copy(way, i - 2).wait_recv()
-                block = block + orecv[way, i - 2]
-            osend[way, i] = block
-            o_copy(way, i).start()
+    def pass_on(way, i):
+        d = 4 - (i + 1) // 2
+        block = part(d if way == 0 else -d, (i % 2) ^ way)
+        if i >= 2:
+            o_copy(way, i - 2).wait_recv()
+            block = block + orecv[way, i - 2]
+        osend[way, i] = block
+        o_copy(way, i).start()
+
+    even = odd == 0
+
+    def passes(steps_even, steps_odd):
+        for now, steps in ((even, steps_even), (jnp.logical_not(even), steps_odd)):
+
+            @pl.when(now)
+            def _(steps=steps):
+                for way, i in steps:
+                    pass_on(way, i)
+
+    @pl.when(c == 1)
+    def _():
+        def take(k, carry):
+            for slot in range(4):
+                q_copy_in(k, slot).wait_recv()
+            return carry
+
+        lax.fori_loop(0, 8, take, 0)
+
+    late = [(way, i) for i in range(3, 7) for way in range(2)]
+    steps = [
+        ([(0, 0), (1, 0), (1, 1)], [(0, 0), (1, 0), (0, 1)]),
+        ([(0, 1), (0, 2), (1, 2)], [(1, 1), (0, 2), (1, 2)]),
+    ]
+    def squares_of(n, carry):
+        offset = jnp.where(n == 0, 2, jnp.where(n == 1, 1 + 2 * odd, jnp.where(n == 2, 3 - 2 * odd, 0)))
+        product(lax.rem(lax.div(z, 2) + offset, 4))
+        for m in range(2):
+            pl.when(n == m)(functools.partial(passes, *steps[m]))
+        return carry
+
+    lax.fori_loop(0, 4, squares_of, 0)
+    for way, i in late:
+        pass_on(way, i)
+
     for i in (5, 6):
         for way in range(2):
             o_copy(way, i).wait_recv()
@@ -256,7 +323,7 @@
             fin_copy(k, way).wait_send()
         for move in range(4):
             r_copy(k, move).wait_send()
-            q_copy(k, move).wait_send()
+            hand_over(k, move, "wait_send")
         return carry
 
     lax.fori_loop(0, 8, sent, 0)
@@ -266,13 +333,11 @@
 
 
 def on_device(token_ids, attn_out, cotangent, basis_in, basis_out):
-    keep_mask = (token_ids != 0).astype(BF16)[:, :, None]
-    masked = (cotangent * keep_mask).reshape(2, 256, 512)
     dma = pltpu.SemaphoreType.DMA
     return pl.pallas_call(
         kernel,
         out_shape=jax.ShapeDtypeStruct((512, 128), F32),
-        in_specs=[pl.BlockSpec(memory_space=pl.ANY)] * 4,
+        in_specs=[pl.BlockSpec(memory_space=pltpu.VMEM)] + [pl.BlockSpec(memory_space=pl.ANY)] * 4,
         out_specs=pl.BlockSpec(memory_space=pltpu.VMEM),
         scratch_shapes=[
             pltpu.VMEM((8, 256, 1024), BF16),
@@ -295,7 +360,7 @@
         compiler_params=pltpu.CompilerParams(
             collective_id=0, has_side_effects=True, vmem_limit_bytes=48 * 1024 * 1024
         ),
-    )(attn_out.reshape(2, 256, 512), masked, basis_in, basis_out)
+    )(token_ids, attn_out.reshape(2, 256, 512), cotangent.reshape(2, 256, 512), basis_in, basis_out)
 
 
 def solution(mesh):

time: 125 us -> 120 us (0.960)
  Pallas kernels: 122 us -> 114 us
  local copies, waits for them, and re-layouts: 0.72 us -> 5.28 us
  other arithmetic: 1.93 us -> 0 us
    pallas_call x1, Pallas kernels: 122 us -> 114 us  [on_device(): pl.pallas_call(kernel, out_shape=jax.ShapeDtypeStruct((512, 128), F32), i...]
    unnamed x7 -> x11, local copies, waits for them, and re-layouts: 0.72 us -> 5.28 us
where the time goes in v2:
time: 120 us
  Pallas kernels  114 us (95%)
  local copies, waits for them, and re-layouts  5.28 us (4%)
    pallas_call x1, Pallas kernels, on_device(): pl.pallas_call(kernel, out_shape=jax.ShapeDtypeStruct((512, 128), F32), i...  114 us
    unnamed x11, local copies, waits for them, and re-layouts  5.28 us

profile of v2, /device:TPU:1, one launch (start us, length us, event | category | flops | bytes accessed | tf_op | source)
XLA Modules:
  0.0 119.6 jit_solution(8753492341946737514)
XLA Ops:
  0.0 0.0 copy-start.4
  0.0 0.7 copy-done.4
  0.7 0.0 copy-start
  0.7 1.0 copy-done
  1.7 0.0 copy-start.1
  1.7 1.0 copy-done.1
  2.8 0.0 copy-start.2
  2.8 0.9 copy-done.2
  3.7 0.0 copy-start.3
  3.7 0.9 copy-done.3
  4.6 114.3 %shard_map.55 = f32[512,128]{1,0:T(8,128)S(1)} custom-call(s32[4,128]{1,0:T(4,128)S(1)} %copy-done.4, bf16[2,256,512]{2,1,0:T(8,128)(2,1)S(1)} %bitcast.2, bf16[2,256,512]{2,1,0:T(8,128)(2,1)S(1)} %bitcast.3, bf16[512,128]{1,0:T(8,128)(2,1)S(1)} %copy-done.2, bf16[512,128]{1,0:T(8,128)(2,1)S(1)} %copy-done.3), custom_call_target="tpu_custom_call" | custom-call | tf_op jit(solution)/shard_map/pallas_call | solution.py:337
  118.9 0.7 copy.7
Async XLA Ops:
  0.0 0.7 copy-start.4
  0.7 1.0 copy-start
  1.7 1.0 copy-start.1
  2.8 0.9 copy-start.2
  3.7 0.9 copy-start.3

commit v3 on v2

--- a/solution.py
+++ b/solution.py
@@ -358,7 +358,7 @@
             dma((2, 7)), dma((2, 7)),
         ],
         compiler_params=pltpu.CompilerParams(
-            collective_id=0, has_side_effects=True, vmem_limit_bytes=48 * 1024 * 1024
+            collective_id=0, has_side_effects=True, vmem_limit_bytes=60 * 1024 * 1024
         ),
     )(token_ids, attn_out.reshape(2, 256, 512), cotangent.reshape(2, 256, 512), basis_in, basis_out)
 

time: 120 us -> 118 us (0.983)
  local copies, waits for them, and re-layouts: 5.28 us -> 1.67 us
  Pallas kernels: 114 us -> 116 us
    unnamed x11 -> x1, local copies, waits for them, and re-layouts: 5.28 us -> 1.67 us
    pallas_call x1, Pallas kernels: 114 us -> 116 us  [on_device(): pl.pallas_call(kernel, out_shape=jax.ShapeDtypeStruct((512, 128), F32), i...]
where the time goes in v3:
time: 118 us
  Pallas kernels  116 us (98%)
  local copies, waits for them, and re-layouts  1.67 us (1%)
    pallas_call x1, Pallas kernels, on_device(): pl.pallas_call(kernel, out_shape=jax.ShapeDtypeStruct((512, 128), F32), i...  116 us

profile of v3, /device:TPU:1, one launch (start us, length us, event | category | flops | bytes accessed | tf_op | source)
XLA Modules:
  0.0 117.5 jit_solution(307115616362164216)
XLA Ops:
  0.0 115.9 %shard_map.55 = f32[512,128]{1,0:T(8,128)} custom-call(s32[4,128]{1,0:T(4,128)} %tokens.1, bf16[2,256,512]{2,1,0:T(8,128)(2,1)} %bitcast.2, bf16[2,256,512]{2,1,0:T(8,128)(2,1)} %bitcast.3, bf16[512,128]{1,0:T(8,128)(2,1)} %b_in.1, bf16[512,128]{1,0:T(8,128)(2,1)} %b_out.1), custom_call_target="tpu_custom_call" | custom-call | tf_op jit(solution)/shard_map/pallas_call | solution.py:337
  115.9 1.7 %copy.7 = f32[512,128]{1,0:T(8,128)} copy(f32[512,128]{1,0:T(8,128)} %shard_map.55) | data formatting | bytes 524288

commit v4 on v3

--- a/solution.py
+++ b/solution.py
@@ -74,22 +74,23 @@
         for copy in swap(cot, b_out, attn, b_in)():
             copy.start()
 
+    def local_b():
+        pltpu.make_async_copy(b_in, b.at[own_pair, half, own_lanes], local_sem.at[2]).wait()
+
     def swapped_b():
-        pltpu.make_async_copy(b_in, b.at[own_pair, half, own_lanes], local_sem.at[2]).wait()
         remote(b_in, b.at[own_pair, other, own_lanes], swap_send.at[2], swap_recv.at[2], partner).wait()
 
     def swapped_a(u):
         pltpu.make_async_copy(attn.at[u], a.at[u, :, half], local_sem.at[u]).wait()
         remote(attn.at[u], a.at[u, :, other], swap_send.at[u], swap_recv.at[u], partner).wait()
 
-    def b_copy(hop, way, receive=False):
+    def b_copy(hop, way, j, receive=False):
         origin = z - hop if way == 0 else z + hop
         if receive:
             origin = origin - 1 if way == 0 else origin + 1
         pair, lanes = b_cols(origin)
-        rows = pl.ds(0, 1024) if hop < 3 else pl.ds(512 * way, 512)
-        block = b.at[pair, rows, lanes]
-        return remote(block, block, b_send.at[hop, way], b_recv.at[hop, way], zr if way == 0 else zl)
+        block = b.at[pair, other if j else half, lanes]
+        return remote(block, block, b_send.at[hop, way, j], b_recv.at[hop, way, j], zr if way == 0 else zl)
 
     a_moves = [(0, 2, 0), (1, 3, 1), (1, 4, 0), (0, 5, 1), (2, 6, 0), (3, 7, 1)]
 
@@ -109,9 +110,12 @@
                 column = jnp.sum(jnp.where(diagonal, keep, 0.0), axis=1, keepdims=True).astype(BF16)
                 a[u, 128 * h : 128 * h + 128, :] = a[u, 128 * h : 128 * h + 128, :] * column
 
+    local_b()
+    for way in range(2):
+        b_copy(0, way, 0).start()
     swapped_b()
     for way in range(2):
-        b_copy(0, way).start()
+        b_copy(0, way, 1).start()
     take_a(0)
     a_copy(0).start()
     take_a(1)
@@ -120,10 +124,12 @@
     a_copy(3).start()
     acc[...] = jnp.zeros_like(acc)
     for hop in range(4):
-        for way in range(2):
-            b_copy(hop, way, receive=True).wait_recv()
-            if hop < 3:
-                b_copy(hop + 1, way).start()
+        for j in range(2):
+            for way in range(2):
+                if hop < 3 or j == way:
+                    b_copy(hop, way, j, receive=True).wait_recv()
+                if hop < 2 or (hop == 2 and j == way):
+                    b_copy(hop + 1, way, j).start()
         if hop == 1:
             for move in range(2):
                 a_copy(move).wait_recv()
@@ -313,7 +319,9 @@
 
     for hop in range(4):
         for way in range(2):
-            b_copy(hop, way).wait_send()
+            for j in range(2):
+                if hop < 3 or j == way:
+                    b_copy(hop, way, j).wait_send()
     for move in range(6):
         a_copy(move).wait_send()
 
@@ -351,7 +359,7 @@
             pltpu.VMEM((2, 7, 256, 128), F32),
             pltpu.VMEM((2, 7, 256, 128), F32),
             dma((3,)), dma((3,)), dma((3,)),
-            dma((4, 2)), dma((4, 2)),
+            dma((4, 2, 2)), dma((4, 2, 2)),
             dma((6,)), dma((8,)),
             dma((8, 2)), dma((8, 2)), dma((8, 2)), dma((8, 2)),
             dma((8, 4)), dma((8, 4)), dma((8, 4)), dma((8, 4)),

time: 118 us -> 114 us (0.966)
  Pallas kernels: 116 us -> 112 us
    pallas_call x1, Pallas kernels: 116 us -> 112 us  [on_device(): pl.pallas_call(kernel, out_shape=jax.ShapeDtypeStruct((512, 128), F32), i...]
where the time goes in v4:
time: 114 us; the launch traced here: 113 us
  Pallas kernels  112 us (98%)
  local copies, waits for them, and re-layouts  1.67 us (1%)
    pallas_call x1, Pallas kernels, on_device(): pl.pallas_call(kernel, out_shape=jax.ShapeDtypeStruct((512, 128), F32), i...  112 us

profile of v4, /device:TPU:1, one launch (start us, length us, event | category | flops | bytes accessed | tf_op | source)
XLA Modules:
  0.0 113.5 jit_solution(15248051886111929511)
XLA Ops:
  0.0 111.8 %shard_map.55 = f32[512,128]{1,0:T(8,128)} custom-call(s32[4,128]{1,0:T(4,128)} %tokens.1, bf16[2,256,512]{2,1,0:T(8,128)(2,1)} %bitcast.2, bf16[2,256,512]{2,1,0:T(8,128)(2,1)} %bitcast.3, bf16[512,128]{1,0:T(8,128)(2,1)} %b_in.1, bf16[512,128]{1,0:T(8,128)(2,1)} %b_out.1), custom_call_target="tpu_custom_call" | custom-call | tf_op jit(solution)/shard_map/pallas_call | solution.py:345
  111.8 1.7 %copy.7 = f32[512,128]{1,0:T(8,128)} copy(f32[512,128]{1,0:T(8,128)} %shard_map.55) | data formatting | bytes 524288

commit v5 on v4

--- a/solution.py
+++ b/solution.py
@@ -130,7 +130,7 @@
                     b_copy(hop, way, j, receive=True).wait_recv()
                 if hop < 2 or (hop == 2 and j == way):
                     b_copy(hop + 1, way, j).start()
-        if hop == 1:
+        if hop == 2:
             for move in range(2):
                 a_copy(move).wait_recv()
                 a_copy(move + 4).start()

time: 114 us -> 114 us (level)
  no operation moved by 1% of the time
where the time goes in v5:
time: 114 us; the launch traced here: 113 us
  Pallas kernels  112 us (98%)
  local copies, waits for them, and re-layouts  1.67 us (1%)
    pallas_call x1, Pallas kernels, on_device(): pl.pallas_call(kernel, out_shape=jax.ShapeDtypeStruct((512, 128), F32), i...  112 us

profile of v5, /device:TPU:1, one launch (start us, length us, event | category | flops | bytes accessed | tf_op | source)
XLA Modules:
  0.0 113.5 jit_solution(6528848552378078133)
XLA Ops:
  0.0 111.8 %shard_map.55 = f32[512,128]{1,0:T(8,128)} custom-call(s32[4,128]{1,0:T(4,128)} %tokens.1, bf16[2,256,512]{2,1,0:T(8,128)(2,1)} %bitcast.2, bf16[2,256,512]{2,1,0:T(8,128)(2,1)} %bitcast.3, bf16[512,128]{1,0:T(8,128)(2,1)} %b_in.1, bf16[512,128]{1,0:T(8,128)(2,1)} %b_out.1), custom_call_target="tpu_custom_call" | custom-call | tf_op jit(solution)/shard_map/pallas_call | solution.py:345
  111.8 1.7 %copy.7 = f32[512,128]{1,0:T(8,128)} copy(f32[512,128]{1,0:T(8,128)} %shard_map.55) | data formatting | bytes 524288
